TPU v7x, 32 devices: a whole 2x2x4 slice. The times are simulated.
32 devices in a mesh: tile: 8 (over z, x), agg: 4 (over y, core).
Axes of the slice: x: 2, y: 2, z: 4, core: 2. Of those that a mesh axis runs over, the one named last changes fastest.
Arguments:
- right_side: float32 [65536, 256], P(('tile', 'agg')), may hold values from -8 to 8
- diag_tiles: float32 [512, 128, 128], P(('tile', 'agg')), may hold values from -1 to 2
- smoother: float32 [512, 128, 128], P(('tile', 'agg')), may hold values from 0 to 1
- coupling_tiles: float32 [1024, 128, 128], P(('tile', 'agg')), may hold values from -0.003125 to 0
- tile_rows: int32 [1024], P(('tile', 'agg')), may hold values from 0 to 15
- tile_cols: int32 [1024], P(('tile', 'agg')), may hold values from 0 to 15
- cross_end: int32 [8, 4, 3, 4, 32], P('tile', 'agg'), may hold values from 0 to 2047
- cross_count: int32 [8, 4, 3, 4], P('tile', 'agg'), may hold values from 0 to 32, as said below
- cross_weight: float32 [8, 4, 3, 4, 32], P('tile', 'agg'), may hold values from 0.1 to 0.3, as said below
- block_agg: int32 [512, 1], P(('tile', 'agg')), may hold values from 0 to 31
- coarse_inverse: float32 [32, 32], P(('tile', 'agg')), may hold values from -1 to 1
Outputs:
- solution: float32 [65536, 256], P(('tile', 'agg'))
Inputs may be any that keep to these rules, and one draw needn't show every extreme that they name: cross_count[t, g, k, h] equals cross_count[t + k - 1, h, 2 - k, g]; it is zero where t + k - 1 lies outside 0..7 and where k = 1 and h = g; some pair of devices of one tile has exactly 32. cross_weight[t, g, k, h, s] equals cross_weight[t + k - 1, h, 2 - k, g, s] wherever both exist.
All inputs are finite; a program needn't handle non-finite values.
Results may differ from a plain program's by a relative error of at most 0.0001.
Values sent between devices are 32-bit elements; how exact they have to be, the bound alone decides.
A program may use at most 64 MiB of HBM per device.

v0:
```python
import functools

import jax
import jax.numpy as jnp
from jax import lax
from jax.experimental import pallas as pl
from jax.experimental.pallas import tpu as pltpu
from jax.sharding import PartitionSpec as P

MESH = pl.DeviceIdType.MESH
F32 = jnp.float32
BF16 = jnp.bfloat16
HIGHEST = lax.Precision.HIGHEST


def split(x):
    hi = x.astype(BF16)
    lo = (x - hi.astype(F32)).astype(BF16)
    return hi, lo


def kernel(
    tiles, owners, nb, nt, blk, dates, cap, nagg,
    ends_s, weight_s, cols_s, prev_s, last_s,
    right_h, diag_h, smooth_h, coup_h,
    ends_v, weight_v, agg_col, agg_row, cinv,
    out_ref,
    right, stage_d, stage_s, stage_c,
    v, vcat, wsm, wop, part, hot, terms, send, recv,
    bsum, partial_ref, red_in, red_sum, all_in, full, ci, corr_rows,
    in_sem, send_sem, recv_sem,
    ra_send, ra_recv, rt_send, rt_recv, rg_send, rg_recv,
    ca_send, ca_recv, ct_send, ct_recv,
):
    t = lax.axis_index("tile")
    g = lax.axis_index("agg")
    slots = 3 * owners * cap
    rows = nagg // owners

    loads = [
        pltpu.make_async_copy(right_h, right, in_sem.at[0]),
        pltpu.make_async_copy(smooth_h, stage_s, in_sem.at[1]),
        pltpu.make_async_copy(diag_h, stage_d, in_sem.at[2]),
        pltpu.make_async_copy(coup_h, stage_c, in_sem.at[3]),
    ]
    for load in loads:
        load.start()

    def section(i):
        k = i // owners
        h = lax.rem(g + lax.rem(i, owners), owners)
        other = t + k - 1
        valid = (other >= 0) & (other < tiles) & jnp.logical_not((k == 1) & (h == g))
        return k, h, other, valid

    barrier = pltpu.get_barrier_semaphore()

    @pl.loop(0, 3 * owners)
    def _(i):
        k, h, other, valid = section(i)

        @pl.when(valid)
        def _():
            pl.semaphore_signal(barrier, inc=1, device_id=(other, h), device_id_type=MESH)

    @pl.loop(1, tiles)
    def _(d):
        pl.semaphore_signal(
            barrier, inc=1, device_id=(lax.rem(t + d, tiles), g), device_id_type=MESH
        )

    @pl.loop(0, 3 * owners)
    def _(i):
        k, h, other, valid = section(i)

        @pl.when(jnp.logical_not(valid))
        def _():
            for turn in range(recv.shape[0]):
                recv[turn, k * owners + h] = jnp.zeros((cap, dates), F32)

    ci[t * owners + g] = jnp.zeros((1, ci.shape[2]), F32)
    ci[t * owners + g, :, 0:nagg] = cinv[...]

    ends = ends_v[...]
    weight = weight_v[...]
    eye = (
        lax.broadcasted_iota(jnp.int32, (blk, blk), 0)
        == lax.broadcasted_iota(jnp.int32, (blk, blk), 1)
    )

    def make_hot(b):
        pick = (lax.broadcasted_iota(jnp.int32, (blk, slots), 0) + b * blk) == ends
        one = jnp.where(pick, 1.0, 0.0).astype(BF16)
        hot[b, :, 0:slots] = one
        hot[b, :, slots : 2 * slots] = one
        return jnp.sum(jnp.where(pick, weight, 0.0), axis=1, keepdims=True)

    def put3(ref, b, x):
        hi, lo = split(x)
        ref[b, 0:blk, :] = hi
        ref[b, blk : 2 * blk, :] = hi
        ref[b, 2 * blk : 3 * blk, :] = lo

    def put3w(ref, b, x):
        hi, lo = split(x)
        ref[b, :, 0:blk] = hi
        ref[b, :, blk : 2 * blk] = lo
        ref[b, :, 2 * blk : 3 * blk] = hi

    def product(w, x):
        return jnp.dot(w, x, preferred_element_type=F32)

    def cat3(x):
        hi, lo = split(x)
        return jnp.concatenate([hi, hi, lo], axis=0)

    loads[0].wait()
    loads[1].wait()

    @pl.loop(0, nb, unroll=2)
    def _(b):
        put3w(wsm, b, stage_s[b])
        new = product(wsm[b], cat3(right[b]))
        v[pl.ds(pl.multiple_of(b * blk, blk), blk), :] = new
        put3(vcat, b, new)

    nvalid = (
        (owners - 1)
        + owners * (t > 0).astype(jnp.int32)
        + owners * (t < tiles - 1).astype(jnp.int32)
    )
    pl.semaphore_wait(barrier, nvalid + tiles - 1)

    def ci_copy_agg(d):
        h = lax.rem(g + d, owners)
        return pltpu.make_async_remote_copy(
            src_ref=ci.at[t * owners + g],
            dst_ref=ci.at[t * owners + g],
            send_sem=ca_send.at[d],
            recv_sem=ca_recv.at[d],
            device_id=(t, h),
            device_id_type=MESH,
        )

    def ci_copy_tile(d):
        return pltpu.make_async_remote_copy(
            src_ref=ci.at[pl.ds(t * owners, owners)],
            dst_ref=ci.at[pl.ds(t * owners, owners)],
            send_sem=ct_send.at[d],
            recv_sem=ct_recv.at[d],
            device_id=(lax.rem(t + d, tiles), g),
            device_id_type=MESH,
        )

    for d in range(1, owners):
        ci_copy_agg(d).start()

    def halo_copy(turn, i):
        k, h, other, valid = section(i)
        return valid, pltpu.make_async_remote_copy(
            src_ref=send.at[turn, i],
            dst_ref=recv.at[turn, (2 - k) * owners + g],
            send_sem=send_sem.at[turn, i],
            recv_sem=recv_sem.at[turn, (2 - k) * owners + g],
            device_id=(other, h),
            device_id_type=MESH,
        )

    def halo_start(turn):
        @pl.loop(0, 3 * owners)
        def _(i):
            k, h, other, valid = section(i)
            base = (k * owners + h) * cap
            for s in range(cap):
                row = v[pl.ds(ends_s[base + s], 1), :]
                send[turn, i, s : s + 1, :] = row * weight_s[base + s]
            _, copy = halo_copy(turn, i)

            @pl.when(valid)
            def _():
                copy.start()

    def halo_finish(turn):
        @pl.loop(0, 3 * owners)
        def _(i):
            k, h, other, valid = section(i)

            @pl.when(valid)
            def _():
                src = k * owners + h
                pltpu.make_async_remote_copy(
                    src_ref=send.at[turn, i],
                    dst_ref=recv.at[turn, src],
                    send_sem=send_sem.at[turn, i],
                    recv_sem=recv_sem.at[turn, src],
                    device_id=(other, h),
                    device_id_type=MESH,
                ).wait()

        @pl.loop(0, 3 * owners)
        def _(i):
            hi, lo = split(recv[turn, i])
            at = pl.multiple_of(i * cap, cap)
            terms[pl.ds(at, cap), :] = hi
            terms[pl.ds(slots + at, cap), :] = lo

    def local_part():
        @pl.loop(0, nb, unroll=4)
        def _(b):
            part[b] = product(wop[b], vcat[b])

        @pl.loop(0, nt, unroll=4)
        def _(c):
            part[nb + c] = part[prev_s[c]] + product(wop[nb + c], vcat[cols_s[c]])

    def residual(b):
        return right[b] - part[last_s[b]] + product(hot[b], terms[...])

    def sweep(final):
        @pl.loop(0, nb, unroll=4)
        def _(b):
            at = pl.ds(pl.multiple_of(b * blk, blk), blk)
            new = v[at, :] + product(wsm[b], cat3(residual(b)))
            if final:
                out_ref[at, :] = new
            else:
                v[at, :] = new
                put3(vcat, b, new)

    halo_start(0)
    loads[2].wait()
    loads[3].wait()

    @pl.loop(0, nb)
    def _(b):
        tail = make_hot(b)
        put3w(wop, b, stage_d[b] + jnp.where(eye, tail, 0.0))

    @pl.loop(0, nt, unroll=2)
    def _(c):
        put3w(wop, nb + c, stage_c[c])

    local_part()
    for d in range(1, owners):
        ci_copy_agg(d).wait()

    @pl.loop(1, tiles)
    def _(d):
        ci_copy_tile(d).start()

    halo_finish(0)
    sweep(False)

    halo_start(1)
    local_part()
    halo_finish(1)

    @pl.loop(0, nb, unroll=4)
    def _(b):
        bsum[pl.ds(b, 1), :] = jnp.sum(residual(b), axis=0, keepdims=True)

    pick_t = jnp.where(
        lax.broadcasted_iota(jnp.int32, (nagg, nb), 0) == agg_row[...], 1.0, 0.0
    )
    partial_ref[...] = jnp.dot(
        pick_t, bsum[...], preferred_element_type=F32, precision=HIGHEST
    )

    def red_copy(d):
        h = lax.rem(g + d, owners)
        return pltpu.make_async_remote_copy(
            src_ref=partial_ref.at[pl.ds(pl.multiple_of(h * rows, rows), rows)],
            dst_ref=red_in.at[d],
            send_sem=ra_send.at[d],
            recv_sem=ra_recv.at[d],
            device_id=(t, h),
            device_id_type=MESH,
        )

    for d in range(1, owners):
        red_copy(d).start()
    total = partial_ref[pl.ds(pl.multiple_of(g * rows, rows), rows), :]
    for d in range(1, owners):
        red_copy(d).wait()
        total = total + red_in[d]
    red_sum[...] = total

    def tile_copy(d):
        return pltpu.make_async_remote_copy(
            src_ref=red_sum,
            dst_ref=all_in.at[d],
            send_sem=rt_send.at[d],
            recv_sem=rt_recv.at[d],
            device_id=(lax.rem(t + d, tiles), g),
            device_id_type=MESH,
        )

    @pl.loop(1, tiles)
    def _(d):
        tile_copy(d).start()

    all_in[0] = red_sum[...]

    @pl.loop(1, tiles)
    def _(d):
        tile_copy(d).wait()

    own_rows = pl.ds(pl.multiple_of(g * rows, rows), rows)
    full[own_rows, :] = jnp.sum(all_in[...], axis=0)

    def gather_copy(d):
        h = lax.rem(g + d, owners)
        return pltpu.make_async_remote_copy(
            src_ref=full.at[own_rows],
            dst_ref=full.at[own_rows],
            send_sem=rg_send.at[d],
            recv_sem=rg_recv.at[d],
            device_id=(t, h),
            device_id_type=MESH,
        )

    for d in range(1, owners):
        gather_copy(d).start()

    @pl.loop(1, tiles)
    def _(d):
        ci_copy_tile(d).wait()

    for d in range(1, owners):
        gather_copy(d).wait()

    inverse = ci[...].reshape(nagg, ci.shape[2])[:, 0:nagg]
    corr = jnp.dot(inverse, full[...], preferred_element_type=F32, precision=HIGHEST)
    pick = jnp.where(
        lax.broadcasted_iota(jnp.int32, (nb, nagg), 1) == agg_col[...], 1.0, 0.0
    )
    corr_rows[...] = jnp.dot(pick, corr, preferred_element_type=F32, precision=HIGHEST)

    @pl.loop(0, nb, unroll=2)
    def _(b):
        at = pl.ds(pl.multiple_of(b * blk, blk), blk)
        new = v[at, :] + corr_rows[pl.ds(b, 1), :]
        v[at, :] = new
        put3(vcat, b, new)

    halo_start(2)
    local_part()
    halo_finish(2)
    sweep(False)
    halo_start(3)
    local_part()
    halo_finish(3)
    sweep(True)


def local(
    tiles, right_side, diag_tiles, smoother, coupling_tiles, tile_rows, tile_cols,
    cross_end, cross_count, cross_weight, block_agg, coarse_inverse,
):
    nb, blk, _ = diag_tiles.shape
    nt = coupling_tiles.shape[0]
    points, dates = right_side.shape
    owners, cap = cross_end.shape[3:]
    nagg = coarse_inverse.shape[1]
    slots = 3 * owners * cap
    rows = nagg // owners
    turns = 4

    ends = cross_end.reshape(slots)
    live = jnp.arange(cap, dtype=jnp.int32) < cross_count[0, 0][:, :, None]
    weight = jnp.where(live, cross_weight[0, 0], 0.0).reshape(slots)
    order = jnp.arange(nt, dtype=jnp.int32)
    same = (tile_rows[:, None] == tile_rows[None, :]) & (order[None, :] < order[:, None])
    prev = jnp.maximum(
        jnp.max(jnp.where(same, order[None, :] + nb, 0), axis=1), tile_rows
    )
    block = jnp.arange(nb, dtype=jnp.int32)
    last = jnp.maximum(
        jnp.max(jnp.where(tile_rows[None, :] == block[:, None], order[None, :] + nb, 0), axis=1),
        block,
    )
    smem = pl.BlockSpec(memory_space=pltpu.SMEM)
    vmem = pl.BlockSpec(memory_space=pltpu.VMEM)
    hbm = pl.BlockSpec(memory_space=pl.ANY)
    dma = pltpu.SemaphoreType.DMA
    return pl.pallas_call(
        functools.partial(kernel, tiles, owners, nb, nt, blk, dates, cap, nagg),
        out_shape=jax.ShapeDtypeStruct((points, dates), F32),
        in_specs=[smem] * 5 + [hbm] * 4 + [vmem] * 5,
        out_specs=vmem,
        scratch_shapes=[
            pltpu.VMEM((nb, blk, dates), F32),
            pltpu.VMEM((nb, blk, blk), F32),
            pltpu.VMEM((nb, blk, blk), F32),
            pltpu.VMEM((nt, blk, blk), F32),
            pltpu.VMEM((points, dates), F32),
            pltpu.VMEM((nb, 3 * blk, dates), BF16),
            pltpu.VMEM((nb, blk, 3 * blk), BF16),
            pltpu.VMEM((nb + nt, blk, 3 * blk), BF16),
            pltpu.VMEM((nb + nt, blk, dates), F32),
            pltpu.VMEM((nb, blk, 2 * slots), BF16),
            pltpu.VMEM((2 * slots, dates), BF16),
            pltpu.VMEM((turns, 3 * owners, cap, dates), F32),
            pltpu.VMEM((turns, 3 * owners, cap, dates), F32),
            pltpu.VMEM((nb, dates), F32),
            pltpu.VMEM((nagg, dates), F32),
            pltpu.VMEM((owners, rows, dates), F32),
            pltpu.VMEM((rows, dates), F32),
            pltpu.VMEM((tiles, rows, dates), F32),
            pltpu.VMEM((nagg, dates), F32),
            pltpu.VMEM((nagg, 1, 128 * ((nagg + 127) // 128)), F32),
            pltpu.VMEM((nb, dates), F32),
            dma((4,)),
            dma((turns, 3 * owners)),
            dma((turns, 3 * owners)),
            dma((owners,)), dma((owners,)),
            dma((tiles,)), dma((tiles,)),
            dma((owners,)), dma((owners,)),
            dma((owners,)), dma((owners,)),
            dma((tiles,)), dma((tiles,)),
        ],
        compiler_params=pltpu.CompilerParams(
            collective_id=0, has_side_effects=True, vmem_limit_bytes=56 * 1024 * 1024
        ),
        cost_estimate=pl.CostEstimate(
            flops=8 * 256 * blk * blk * dates, bytes_accessed=8 << 20, transcendentals=0
        ),
    )(
        ends, weight, tile_cols, prev, last,
        right_side.reshape(nb, blk, dates), diag_tiles, smoother, coupling_tiles,
        ends.reshape(1, slots), weight.reshape(1, slots),
        block_agg, block_agg.reshape(1, nb), coarse_inverse,
    )


def solution(mesh):
    both = ("tile", "agg")
    placed = (
        P(both, None),
        P(both, None, None),
        P(both, None, None),
        P(both, None, None),
        P(both),
        P(both),
        P("tile", "agg", None, None, None),
        P("tile", "agg", None, None),
        P("tile", "agg", None, None, None),
        P(both, None),
        P(both, None),
    )
    return jax.shard_map(
        functools.partial(local, mesh.shape["tile"]),
        mesh=mesh, in_specs=placed, out_specs=P(both, None), check_vma=False,
    )
```

profile of v0, /device:TPU:0, one launch (start us, length us, event | category | flops | bytes accessed | tf_op | source)
XLA Modules:
  0.0 82.5 jit_solution(3689288179355075678)
XLA Ops:
  0.0 0.8 select_reduce_fusion.1
  0.8 0.9 %select_reduce_fusion = s32[32]{0:T(128)S(1)} fusion(s32[32]{0:T(128)S(1)} %iota_add_fusion, s32[32]{0:T(128)} %param.15), kind=kLoop, calls=%fused_computation | loop fusion | flops 5088 | bytes 384 | tf_op jit(solution)/shard_map/reduce_max | solution.py:375
  1.7 1.2 %max.6.prev_s = s32[32]{0:T(128)} maximum(s32[32]{0:T(128)S(1)} %select_reduce_fusion, s32[32]{0:T(128)} %param.15) | non-fusion elementwise | flops 32 | bytes 384 | tf_op jit(solution)/shard_map/max | solution.py:374
  2.9 0.5 iota_maximum_fusion.last_s
  3.4 1.4 %reshape_reshape.4.ends_v = s32[1,384]{1,0:T(1,128)} reshape(s32[1,1,3,4,32]{4,3,2,1,0:T(4,128)} %param.17) | data formatting | bytes 3072 | tf_op jit(solution)/shard_map/reshape;reshape | solution.py:431
  4.8 0.8 squeeze.6
  5.6 0.7 copy.16
  6.3 0.1 iota_compare_fusion.2
  6.3 0.1 lt.46
  6.4 0.1 lt.50
  6.5 0.5 broadcast_select_fusion.1.weight_v
  7.0 1.4 %reshape.54.ends_s = s32[384]{0:T(512)} reshape(s32[1,1,3,4,32]{4,3,2,1,0:T(4,128)} %param.17) | data formatting | bytes 3072 | tf_op jit(solution)/shard_map/reshape | solution.py:369
  8.4 0.8 squeeze.5
  9.2 0.6 broadcast_select_fusion.weight_s
  9.8 1.3 %copy.13.agg_col = s32[16,1]{1,0:T(8,128)} copy(s32[16,1]{0,1:T(1,128)} %param.20) | data formatting | bytes 128 | tf_op args[9]
  11.1 68.4 %shard_map.109 = f32[2048,256]{1,0:T(8,128)} custom-call(s32[384]{0:T(512)} %reshape.54.ends_s, f32[384]{0:T(512)} %broadcast_select_fusion.weight_s, s32[32]{0:T(128)} %cols_s.1, s32[32]{0:T(128)} %max.6.prev_s, s32[16]{0:T(128)} %iota_maximum_fusion.last_s, f32[16,128,256]{2,1,0:T(8,128)} %bitcast.7, f32[16,128,128]{2,1,0:T(8,128)} %diag_h.1, ...), custom_call_target="tpu_custom_call" | custom-call | flops 8589934592 | bytes 8388608 | tf_op jit(solution)/shard_map/pallas_call | solution.py:386
  79.5 3.0 %copy.18 = f32[2048,256]{1,0:T(8,128)} copy(f32[2048,256]{1,0:T(8,128)} %shard_map.109) | data formatting | bytes 4194304
  (1 shorter events, 0.0 us)
where the time goes:
time: 83.5 us; the launch traced here: 82.5 us
  Pallas kernels  68.4 us (82%)
  local copies, waits for them, and re-layouts  9.51 us (11%)
  other arithmetic  4.62 us (6%)
    pallas_call x1, Pallas kernels, local(): pl.pallas_call(functools.partial(kernel, tiles, owners, nb, nt, blk, date...  68.4 us
    unnamed x3, local copies, waits for them, and re-layouts  5.06 us

commit v1 on v0

--- a/solution.py
+++ b/solution.py
@@ -21,14 +21,15 @@
 
 def kernel(
     tiles, owners, nb, nt, blk, dates, cap, nagg,
-    ends_s, weight_s, cols_s, prev_s, last_s,
+    ends_s, count_s, raw_s, rows_s, cols_s, agg_s,
     right_h, diag_h, smooth_h, coup_h,
-    ends_v, weight_v, agg_col, agg_row, cinv,
+    ends_v, raw_v, agg_row, cinv,
     out_ref,
     right, stage_d, stage_s, stage_c,
     v, vcat, wsm, wop, part, hot, terms, send, recv,
-    bsum, partial_ref, red_in, red_sum, all_in, full, ci, corr_rows,
-    in_sem, send_sem, recv_sem,
+    bsum, partial_ref, red_in, red_sum, all_in, full, ci, corr_ref,
+    ends_row, weight_row, prev_s, last_s, resid, flat, ap3, corr3, send_p, recv_p,
+    in_sem, send_sem, recv_sem, psend_sem, precv_sem,
     ra_send, ra_recv, rt_send, rt_recv, rg_send, rg_recv,
     ca_send, ca_recv, ct_send, ct_recv,
 ):
@@ -36,6 +37,7 @@
     g = lax.axis_index("agg")
     slots = 3 * owners * cap
     rows = nagg // owners
+    lanes = recv_p.shape[2]
 
     loads = [
         pltpu.make_async_copy(right_h, right, in_sem.at[0]),
@@ -77,12 +79,35 @@
         def _():
             for turn in range(recv.shape[0]):
                 recv[turn, k * owners + h] = jnp.zeros((cap, dates), F32)
+            recv_p[k * owners + h] = jnp.zeros((cap, lanes), F32)
 
     ci[t * owners + g] = jnp.zeros((1, ci.shape[2]), F32)
     ci[t * owners + g, :, 0:nagg] = cinv[...]
 
-    ends = ends_v[...]
-    weight = weight_v[...]
+    for k in range(3):
+        for h in range(owners):
+            at = (k * owners + h) * cap
+            ends_row[:, at : at + cap] = ends_v[0, 0, k, h : h + 1, :]
+            alive = lax.broadcasted_iota(jnp.int32, (1, cap), 1) < count_s[0, 0, k, h]
+            weight_row[:, at : at + cap] = jnp.where(alive, raw_v[0, 0, k, h : h + 1, :], 0.0)
+
+    @pl.loop(0, nt)
+    def _(c):
+        row = rows_s[c]
+        found = row
+        for e in range(nt):
+            found = jnp.where((rows_s[e] == row) & (e < c), nb + e, found)
+        prev_s[c] = found
+
+    @pl.loop(0, nb)
+    def _(b):
+        found = b
+        for e in range(nt):
+            found = jnp.where(rows_s[e] == b, nb + e, found)
+        last_s[b] = found
+
+    ends = ends_row[...]
+    weight = weight_row[...]
     eye = (
         lax.broadcasted_iota(jnp.int32, (blk, blk), 0)
         == lax.broadcasted_iota(jnp.int32, (blk, blk), 1)
@@ -170,15 +195,84 @@
         @pl.loop(0, 3 * owners)
         def _(i):
             k, h, other, valid = section(i)
-            base = (k * owners + h) * cap
+            count = count_s[0, 0, k, h]
             for s in range(cap):
-                row = v[pl.ds(ends_s[base + s], 1), :]
-                send[turn, i, s : s + 1, :] = row * weight_s[base + s]
+                end = ends_s[0, 0, k, h, s]
+                scale = jnp.where(s < count, raw_s[0, 0, k, h, s], 0.0)
+                send[turn, i, s : s + 1, :] = v[pl.ds(end, 1), :] * scale
             _, copy = halo_copy(turn, i)
 
             @pl.when(valid)
             def _():
                 copy.start()
+
+    def basis_copy(i):
+        k, h, other, valid = section(i)
+        return pltpu.make_async_remote_copy(
+            src_ref=send_p.at[i],
+            dst_ref=recv_p.at[(2 - k) * owners + g],
+            send_sem=psend_sem.at[i],
+            recv_sem=precv_sem.at[(2 - k) * owners + g],
+            device_id=(other, h),
+            device_id_type=MESH,
+        )
+
+    def basis_start():
+        lane = lax.broadcasted_iota(jnp.int32, (1, lanes), 1)
+
+        @pl.loop(0, 3 * owners)
+        def _(i):
+            k, h, other, valid = section(i)
+            count = count_s[0, 0, k, h]
+            for s in range(cap):
+                target = agg_s[0, lax.div(ends_s[0, 0, k, h, s], blk)]
+                scale = jnp.where(s < count, raw_s[0, 0, k, h, s], 0.0)
+                send_p[i, s : s + 1, :] = jnp.where(lane == target, scale, 0.0)
+
+            @pl.when(valid)
+            def _():
+                basis_copy(i).start()
+
+    def basis_finish():
+        @pl.loop(0, 3 * owners)
+        def _(i):
+            k, h, other, valid = section(i)
+
+            @pl.when(valid)
+            def _():
+                src = k * owners + h
+                pltpu.make_async_remote_copy(
+                    src_ref=send_p.at[i],
+                    dst_ref=recv_p.at[src],
+                    send_sem=psend_sem.at[i],
+                    recv_sem=precv_sem.at[src],
+                    device_id=(other, h),
+                    device_id_type=MESH,
+                ).wait()
+
+        lane = lax.broadcasted_iota(jnp.int32, (1, lanes), 1)
+
+        @pl.loop(0, nb, unroll=2)
+        def _(b):
+            total = jnp.sum(stage_d[b], axis=1, keepdims=True)
+            flat[b] = jnp.where(lane == agg_s[0, b], total, 0.0)
+
+        @pl.loop(0, nt, unroll=2)
+        def _(c):
+            total = jnp.sum(stage_c[c], axis=1, keepdims=True)
+            flat[nb + c] = flat[prev_s[c]] + jnp.where(
+                lane == agg_s[0, cols_s[c]], total, 0.0
+            )
+
+        hi, lo = split(recv_p[...].reshape(slots, lanes))
+        heads = jnp.concatenate([hi, lo], axis=0)
+
+        @pl.loop(0, nb, unroll=2)
+        def _(b):
+            hi, lo = split(flat[last_s[b]] - product(hot[b], heads))
+            ap3[b, :, 0:lanes] = hi
+            ap3[b, :, lanes : 2 * lanes] = lo
+            ap3[b, :, 2 * lanes : 3 * lanes] = hi
 
     def halo_finish(turn):
         @pl.loop(0, 3 * owners)
@@ -234,7 +328,9 @@
     @pl.loop(0, nb)
     def _(b):
         tail = make_hot(b)
-        put3w(wop, b, stage_d[b] + jnp.where(eye, tail, 0.0))
+        tile = stage_d[b] + jnp.where(eye, tail, 0.0)
+        stage_d[b] = tile
+        put3w(wop, b, tile)
 
     @pl.loop(0, nt, unroll=2)
     def _(c):
@@ -252,12 +348,15 @@
     sweep(False)
 
     halo_start(1)
+    basis_start()
     local_part()
     halo_finish(1)
 
     @pl.loop(0, nb, unroll=4)
     def _(b):
-        bsum[pl.ds(b, 1), :] = jnp.sum(residual(b), axis=0, keepdims=True)
+        rest = residual(b)
+        resid[b] = rest
+        bsum[pl.ds(b, 1), :] = jnp.sum(rest, axis=0, keepdims=True)
 
     pick_t = jnp.where(
         lax.broadcasted_iota(jnp.int32, (nagg, nb), 0) == agg_row[...], 1.0, 0.0
@@ -279,6 +378,7 @@
 
     for d in range(1, owners):
         red_copy(d).start()
+    basis_finish()
     total = partial_ref[pl.ds(pl.multiple_of(g * rows, rows), rows), :]
     for d in range(1, owners):
         red_copy(d).wait()
@@ -331,25 +431,21 @@
 
     inverse = ci[...].reshape(nagg, ci.shape[2])[:, 0:nagg]
     corr = jnp.dot(inverse, full[...], preferred_element_type=F32, precision=HIGHEST)
-    pick = jnp.where(
-        lax.broadcasted_iota(jnp.int32, (nb, nagg), 1) == agg_col[...], 1.0, 0.0
-    )
-    corr_rows[...] = jnp.dot(pick, corr, preferred_element_type=F32, precision=HIGHEST)
-
-    @pl.loop(0, nb, unroll=2)
+    corr_ref[...] = jnp.zeros_like(corr_ref)
+    corr_ref[0:nagg, :] = corr
+    corr3[...] = cat3(corr_ref[...])
+
+    @pl.loop(0, nb, unroll=4)
     def _(b):
         at = pl.ds(pl.multiple_of(b * blk, blk), blk)
-        new = v[at, :] + corr_rows[pl.ds(b, 1), :]
+        rest = resid[b] - product(ap3[b], corr3[...])
+        new = v[at, :] + corr_ref[pl.ds(agg_s[0, b], 1), :] + product(wsm[b], cat3(rest))
         v[at, :] = new
         put3(vcat, b, new)
 
     halo_start(2)
     local_part()
     halo_finish(2)
-    sweep(False)
-    halo_start(3)
-    local_part()
-    halo_finish(3)
     sweep(True)
 
 
@@ -364,21 +460,9 @@
     nagg = coarse_inverse.shape[1]
     slots = 3 * owners * cap
     rows = nagg // owners
-    turns = 4
-
-    ends = cross_end.reshape(slots)
-    live = jnp.arange(cap, dtype=jnp.int32) < cross_count[0, 0][:, :, None]
-    weight = jnp.where(live, cross_weight[0, 0], 0.0).reshape(slots)
-    order = jnp.arange(nt, dtype=jnp.int32)
-    same = (tile_rows[:, None] == tile_rows[None, :]) & (order[None, :] < order[:, None])
-    prev = jnp.maximum(
-        jnp.max(jnp.where(same, order[None, :] + nb, 0), axis=1), tile_rows
-    )
-    block = jnp.arange(nb, dtype=jnp.int32)
-    last = jnp.maximum(
-        jnp.max(jnp.where(tile_rows[None, :] == block[:, None], order[None, :] + nb, 0), axis=1),
-        block,
-    )
+    turns = 3
+    lanes = 128 * ((nagg + 127) // 128)
+
     smem = pl.BlockSpec(memory_space=pltpu.SMEM)
     vmem = pl.BlockSpec(memory_space=pltpu.VMEM)
     hbm = pl.BlockSpec(memory_space=pl.ANY)
@@ -386,7 +470,7 @@
     return pl.pallas_call(
         functools.partial(kernel, tiles, owners, nb, nt, blk, dates, cap, nagg),
         out_shape=jax.ShapeDtypeStruct((points, dates), F32),
-        in_specs=[smem] * 5 + [hbm] * 4 + [vmem] * 5,
+        in_specs=[smem] * 6 + [hbm] * 4 + [vmem] * 4,
         out_specs=vmem,
         scratch_shapes=[
             pltpu.VMEM((nb, blk, dates), F32),
@@ -408,11 +492,23 @@
             pltpu.VMEM((rows, dates), F32),
             pltpu.VMEM((tiles, rows, dates), F32),
             pltpu.VMEM((nagg, dates), F32),
-            pltpu.VMEM((nagg, 1, 128 * ((nagg + 127) // 128)), F32),
-            pltpu.VMEM((nb, dates), F32),
+            pltpu.VMEM((nagg, 1, lanes), F32),
+            pltpu.VMEM((lanes, dates), F32),
+            pltpu.VMEM((1, slots), jnp.int32),
+            pltpu.VMEM((1, slots), F32),
+            pltpu.SMEM((nt,), jnp.int32),
+            pltpu.SMEM((nb,), jnp.int32),
+            pltpu.VMEM((nb, blk, dates), F32),
+            pltpu.VMEM((nb + nt, blk, lanes), F32),
+            pltpu.VMEM((nb, blk, 3 * lanes), BF16),
+            pltpu.VMEM((3 * lanes, dates), BF16),
+            pltpu.VMEM((3 * owners, cap, lanes), F32),
+            pltpu.VMEM((3 * owners, cap, lanes), F32),
             dma((4,)),
             dma((turns, 3 * owners)),
             dma((turns, 3 * owners)),
+            dma((3 * owners,)),
+            dma((3 * owners,)),
             dma((owners,)), dma((owners,)),
             dma((tiles,)), dma((tiles,)),
             dma((owners,)), dma((owners,)),
@@ -426,10 +522,9 @@
             flops=8 * 256 * blk * blk * dates, bytes_accessed=8 << 20, transcendentals=0
         ),
     )(
-        ends, weight, tile_cols, prev, last,
+        cross_end, cross_count, cross_weight, tile_rows, tile_cols, block_agg.reshape(1, nb),
         right_side.reshape(nb, blk, dates), diag_tiles, smoother, coupling_tiles,
-        ends.reshape(1, slots), weight.reshape(1, slots),
-        block_agg, block_agg.reshape(1, nb), coarse_inverse,
+        cross_end, cross_weight, block_agg.reshape(1, nb), coarse_inverse,
     )
 
 

time: 83.5 us -> 68 us (0.81)
  Pallas kernels: 68.4 us -> 63.1 us
  local copies, waits for them, and re-layouts: 9.51 us -> 4.3 us
  other arithmetic: 4.62 us -> 0 us
    pallas_call x1, Pallas kernels: 68.4 us -> 63.1 us  [local(): pl.pallas_call(functools.partial(kernel, tiles, owners, nb, nt, blk, date...]
    max x2 -> x0, other arithmetic: 1.75 us -> none  [the longest x1 1.23 us: local(): jnp.maximum(jnp.max(jnp.where(same, order[None, :] + nb, 0), axis=1), til...]
    reduce_max x2 -> x0, other arithmetic: 1.69 us -> none  [the longest x1 0.91 us: local(): jnp.max(jnp.where(same, order[None, :] + nb, 0), axis=1)]
    squeeze x2 -> x0, local copies, waits for them, and re-layouts: 1.55 us -> none  [local(): weight = jnp.where(live, cross_weight[0, 0], 0.0).reshape(slots)]
    reshape x1 -> x0, local copies, waits for them, and re-layouts: 1.37 us -> none  [local(): ends = cross_end.reshape(slots)]
    another operation x1 -> x0, local copies, waits for them, and re-layouts: 1.37 us -> none  [local(): ends.reshape(1, slots)]
    select_n x2 -> x0, other arithmetic: 1.11 us -> none  [local(): weight = jnp.where(live, cross_weight[0, 0], 0.0).reshape(slots)]
    unnamed x3 -> x2, local copies, waits for them, and re-layouts: 5.06 us -> 4.3 us
where the time goes in v1:
time: 68 us; the launch traced here: 67.5 us
  Pallas kernels  63.1 us (93%)
  local copies, waits for them, and re-layouts  4.3 us (6%)
    pallas_call x1, Pallas kernels, local(): pl.pallas_call(functools.partial(kernel, tiles, owners, nb, nt, blk, date...  63.1 us
    unnamed x2, local copies, waits for them, and re-layouts  4.3 us

profile of v1, /device:TPU:0, one launch (start us, length us, event | category | flops | bytes accessed | tf_op | source)
XLA Modules:
  0.0 67.5 jit_solution(5414457741356716430)
XLA Ops:
  0.0 1.3 %copy.12.count_s = s32[1,1,3,4]{3,2,1,0:T(4,128)} copy(s32[1,1,3,4]{3,1,2,0:T(1,128)} %param.18) | data formatting | bytes 96 | tf_op args[7]
  1.3 63.1 %shard_map.109 = f32[2048,256]{1,0:T(8,128)} custom-call(s32[1,1,3,4,32]{4,3,2,1,0:T(4,128)} %ends_v.1, s32[1,1,3,4]{3,2,1,0:T(4,128)} %copy.12.count_s, f32[1,1,3,4,32]{4,3,2,1,0:T(4,128)} %raw_v.1, s32[32]{0:T(128)} %rows_s.1, s32[32]{0:T(128)} %cols_s.1, s32[1,16]{1,0:T(1,128)} %bitcast.3, f32[16,128,256]{2,1,0:T(8,128)} %bitcast.2, ...), custom_call_target="tpu_custom_call" | custom-call | flops 8589934592 | bytes 8388608 | tf_op jit(solution)/shard_map/pallas_call | solution.py:470
  64.4 3.0 %copy.14 = f32[2048,256]{1,0:T(8,128)} copy(f32[2048,256]{1,0:T(8,128)} %shard_map.109) | data formatting | bytes 4194304

commit v2 on v1

--- a/solution.py
+++ b/solution.py
@@ -267,12 +267,15 @@
         hi, lo = split(recv_p[...].reshape(slots, lanes))
         heads = jnp.concatenate([hi, lo], axis=0)
 
-        @pl.loop(0, nb, unroll=2)
-        def _(b):
-            hi, lo = split(flat[last_s[b]] - product(hot[b], heads))
-            ap3[b, :, 0:lanes] = hi
-            ap3[b, :, lanes : 2 * lanes] = lo
-            ap3[b, :, 2 * lanes : 3 * lanes] = hi
+        @pl.loop(0, nb // group)
+        def _(step):
+            arcs = scattered(step * group, heads)
+            for i in range(group):
+                b = step * group + i
+                hi, lo = split(flat[last_s[b]] - arcs[i * blk : (i + 1) * blk])
+                ap3[b, :, 0:lanes] = hi
+                ap3[b, :, lanes : 2 * lanes] = lo
+                ap3[b, :, 2 * lanes : 3 * lanes] = hi
 
     def halo_finish(turn):
         @pl.loop(0, 3 * owners)
@@ -299,27 +302,41 @@
             terms[pl.ds(slots + at, cap), :] = lo
 
     def local_part():
-        @pl.loop(0, nb, unroll=4)
+        @pl.loop(0, nb, unroll=8)
         def _(b):
             part[b] = product(wop[b], vcat[b])
 
-        @pl.loop(0, nt, unroll=4)
+        @pl.loop(0, nt, unroll=8)
         def _(c):
             part[nb + c] = part[prev_s[c]] + product(wop[nb + c], vcat[cols_s[c]])
 
-    def residual(b):
-        return right[b] - part[last_s[b]] + product(hot[b], terms[...])
+    group = 8 if nb % 8 == 0 else 1
+
+    def scattered(first, source):
+        rows_hot = hot[pl.ds(first, group)].reshape(group * blk, 2 * slots)
+        return product(rows_hot, source)
+
+    def residuals(first):
+        arcs = scattered(first, terms[...])
+        return [
+            right[first + i] - part[last_s[first + i]] + arcs[i * blk : (i + 1) * blk]
+            for i in range(group)
+        ]
 
     def sweep(final):
-        @pl.loop(0, nb, unroll=4)
-        def _(b):
-            at = pl.ds(pl.multiple_of(b * blk, blk), blk)
-            new = v[at, :] + product(wsm[b], cat3(residual(b)))
-            if final:
-                out_ref[at, :] = new
-            else:
-                v[at, :] = new
-                put3(vcat, b, new)
+        @pl.loop(0, nb // group)
+        def _(step):
+            first = step * group
+            rests = residuals(first)
+            for i in range(group):
+                b = first + i
+                at = pl.ds(pl.multiple_of(b * blk, blk), blk)
+                new = v[at, :] + product(wsm[b], cat3(rests[i]))
+                if final:
+                    out_ref[at, :] = new
+                else:
+                    v[at, :] = new
+                    put3(vcat, b, new)
 
     halo_start(0)
     loads[2].wait()
@@ -352,11 +369,13 @@
     local_part()
     halo_finish(1)
 
-    @pl.loop(0, nb, unroll=4)
-    def _(b):
-        rest = residual(b)
-        resid[b] = rest
-        bsum[pl.ds(b, 1), :] = jnp.sum(rest, axis=0, keepdims=True)
+    @pl.loop(0, nb // group)
+    def _(step):
+        rests = residuals(step * group)
+        for i in range(group):
+            b = step * group + i
+            resid[b] = rests[i]
+            bsum[pl.ds(b, 1), :] = jnp.sum(rests[i], axis=0, keepdims=True)
 
     pick_t = jnp.where(
         lax.broadcasted_iota(jnp.int32, (nagg, nb), 0) == agg_row[...], 1.0, 0.0

time: 68 us -> 61 us (0.90)
  Pallas kernels: 63.1 us -> 56.5 us
    pallas_call x1, Pallas kernels: 63.1 us -> 56.5 us  [local(): pl.pallas_call(functools.partial(kernel, tiles, owners, nb, nt, blk, date...]
where the time goes in v2:
time: 61 us; the launch traced here: 60.8 us
  Pallas kernels  56.5 us (93%)
  local copies, waits for them, and re-layouts  4.3 us (7%)
    pallas_call x1, Pallas kernels, local(): pl.pallas_call(functools.partial(kernel, tiles, owners, nb, nt, blk, date...  56.5 us
    unnamed x2, local copies, waits for them, and re-layouts  4.3 us

profile of v2, /device:TPU:0, one launch (start us, length us, event | category | flops | bytes accessed | tf_op | source)
XLA Modules:
  0.0 60.8 jit_solution(682421867375422447)
XLA Ops:
  0.0 1.3 %copy.12.count_s = s32[1,1,3,4]{3,2,1,0:T(4,128)} copy(s32[1,1,3,4]{3,1,2,0:T(1,128)} %param.18) | data formatting | bytes 96 | tf_op args[7]
  1.3 56.5 %shard_map.109 = f32[2048,256]{1,0:T(8,128)} custom-call(s32[1,1,3,4,32]{4,3,2,1,0:T(4,128)} %ends_v.1, s32[1,1,3,4]{3,2,1,0:T(4,128)} %copy.12.count_s, f32[1,1,3,4,32]{4,3,2,1,0:T(4,128)} %raw_v.1, s32[32]{0:T(128)} %rows_s.1, s32[32]{0:T(128)} %cols_s.1, s32[1,16]{1,0:T(1,128)} %bitcast.3, f32[16,128,256]{2,1,0:T(8,128)} %bitcast.2, ...), custom_call_target="tpu_custom_call" | custom-call | flops 8589934592 | bytes 8388608 | tf_op jit(solution)/shard_map/pallas_call | solution.py:489
  57.8 3.0 %copy.14 = f32[2048,256]{1,0:T(8,128)} copy(f32[2048,256]{1,0:T(8,128)} %shard_map.109) | data formatting | bytes 4194304

commit v3 on v2

--- a/solution.py
+++ b/solution.py
@@ -142,7 +142,7 @@
     loads[0].wait()
     loads[1].wait()
 
-    @pl.loop(0, nb, unroll=2)
+    @pl.loop(0, nb, unroll=8)
     def _(b):
         put3w(wsm, b, stage_s[b])
         new = product(wsm[b], cat3(right[b]))
@@ -302,11 +302,11 @@
             terms[pl.ds(slots + at, cap), :] = lo
 
     def local_part():
-        @pl.loop(0, nb, unroll=8)
+        @pl.loop(0, nb, unroll=16)
         def _(b):
             part[b] = product(wop[b], vcat[b])
 
-        @pl.loop(0, nt, unroll=8)
+        @pl.loop(0, nt, unroll=16)
         def _(c):
             part[nb + c] = part[prev_s[c]] + product(wop[nb + c], vcat[cols_s[c]])
 
@@ -342,7 +342,7 @@
     loads[2].wait()
     loads[3].wait()
 
-    @pl.loop(0, nb)
+    @pl.loop(0, nb, unroll=2)
     def _(b):
         tail = make_hot(b)
         tile = stage_d[b] + jnp.where(eye, tail, 0.0)
@@ -454,7 +454,7 @@
     corr_ref[0:nagg, :] = corr
     corr3[...] = cat3(corr_ref[...])
 
-    @pl.loop(0, nb, unroll=4)
+    @pl.loop(0, nb, unroll=8)
     def _(b):
         at = pl.ds(pl.multiple_of(b * blk, blk), blk)
         rest = resid[b] - product(ap3[b], corr3[...])

time: 61 us -> 59.1 us (0.969)
  Pallas kernels: 56.5 us -> 54.5 us
    pallas_call x1, Pallas kernels: 56.5 us -> 54.5 us  [local(): pl.pallas_call(functools.partial(kernel, tiles, owners, nb, nt, blk, date...]
where the time goes in v3:
time: 59.1 us; the launch traced here: 58.8 us
  Pallas kernels  54.5 us (92%)
  local copies, waits for them, and re-layouts  4.3 us (7%)
    pallas_call x1, Pallas kernels, local(): pl.pallas_call(functools.partial(kernel, tiles, owners, nb, nt, blk, date...  54.5 us
    unnamed x2, local copies, waits for them, and re-layouts  4.3 us

profile of v3, /device:TPU:0, one launch (start us, length us, event | category | flops | bytes accessed | tf_op | source)
XLA Modules:
  0.0 58.8 jit_solution(3887223608542185724)
XLA Ops:
  0.0 1.3 %copy.12.count_s = s32[1,1,3,4]{3,2,1,0:T(4,128)} copy(s32[1,1,3,4]{3,1,2,0:T(1,128)} %param.18) | data formatting | bytes 96 | tf_op args[7]
  1.3 54.5 %shard_map.109 = f32[2048,256]{1,0:T(8,128)} custom-call(s32[1,1,3,4,32]{4,3,2,1,0:T(4,128)} %ends_v.1, s32[1,1,3,4]{3,2,1,0:T(4,128)} %copy.12.count_s, f32[1,1,3,4,32]{4,3,2,1,0:T(4,128)} %raw_v.1, s32[32]{0:T(128)} %rows_s.1, s32[32]{0:T(128)} %cols_s.1, s32[1,16]{1,0:T(1,128)} %bitcast.3, f32[16,128,256]{2,1,0:T(8,128)} %bitcast.2, ...), custom_call_target="tpu_custom_call" | custom-call | flops 8589934592 | bytes 8388608 | tf_op jit(solution)/shard_map/pallas_call | solution.py:489
  55.8 3.0 %copy.14 = f32[2048,256]{1,0:T(8,128)} copy(f32[2048,256]{1,0:T(8,128)} %shard_map.109) | data formatting | bytes 4194304
